TPU v7x, 32 devices: a whole 2x2x4 slice. The times are simulated.
32 devices in a mesh: rows: 16 (over z, y, core), maps: 2 (over x).
Axes of the slice: x: 2, y: 2, z: 4, core: 2. Of those that a mesh axis runs over, the one named last changes fastest.
Arguments:
- counts: int32 [8, 256, 32768], P(None, 'rows', 'maps'), may hold values from 0 to 2999, as said below
- weights: float32 [8], replicated, may hold values from 0.2 to 5
Outputs:
- barycenter: float32 [256, 32768], P('rows', 'maps')
Inputs may be any that keep to these rules, and one draw needn't show every extreme that they name: `counts`: each count is drawn evenly below a ceiling that grows with the row from 1000 (first row) to 3000 (last row), times a level of 1 to 4 over 4 that is drawn for each run of 64 columns; the largest count, 2999, is reached in every draw.
All inputs are finite; a program needn't handle non-finite values.
Results may differ from a plain program's by a relative error of at most 0.0001.
Values sent between devices are 32-bit elements; how exact they have to be, the bound alone decides.
A program may use at most 128 MiB of HBM per device.

v0:
```python
import jax
import jax.numpy as jnp
from jax import lax
from jax.sharding import PartitionSpec as P

HALF = 8
BLOCK = 256
ITERS = 2


def padded_2(value, sides, width):
    for axis, dim in sides:
        devices, length = (lax.axis_size(axis), value.shape[dim])
        up = [(i, (i + 1) % devices) for i in range(devices - 1)]
        down = [(j, i) for i, j in up]
        last = lax.slice_in_dim(value, length - width, length, axis=dim)
        first = lax.slice_in_dim(value, 0, width, axis=dim)
        before = lax.ppermute(last, axis, up)
        after = lax.ppermute(first, axis, down)
        value = jnp.concatenate([before, value, after], axis=dim)
    return value


def kernel_table(count_out, count_in):
    out_pos = lax.broadcasted_iota(jnp.int32, (count_out, count_in), 0)
    in_pos = lax.broadcasted_iota(jnp.int32, (count_out, count_in), 1)
    offset = in_pos - HALF - out_pos
    spread = 0.45 * HALF
    distance = offset.astype(jnp.float32)
    shape_taps = jnp.exp(-distance * distance / (2.0 * spread * spread))
    across = jnp.arange(-HALF, HALF + 1).astype(jnp.float32)
    tap_total = jnp.sum(jnp.exp(-across * across / (2.0 * spread * spread)))
    return jnp.where(jnp.abs(offset) <= HALF, shape_taps, 0.0) / tap_total


def row_pass(padded, row_count):
    kernel_rows = kernel_table(row_count, row_count + 2 * HALF)
    return jnp.einsum("ij,mjc->mic", kernel_rows, padded, precision=lax.Precision.HIGHEST)


def column_pass(grid_field, left_rim, right_rim):
    leading = grid_field.shape[:-1]
    block_count = grid_field.shape[-1] // BLOCK
    blocks = grid_field.reshape(leading + (block_count, BLOCK))
    block_tails = blocks[..., :, BLOCK - HALF :]
    block_heads = blocks[..., :, :HALF]
    before = jnp.concatenate([left_rim[..., None, :], block_tails[..., :-1, :]], axis=-2)
    following = jnp.concatenate([block_heads[..., 1:, :], right_rim[..., None, :]], axis=-2)
    extended = jnp.concatenate([before, blocks, following], axis=-1)
    kernel_cols = kernel_table(BLOCK, BLOCK + 2 * HALF)
    result = jnp.einsum("mrbj,dj->mrbd", extended, kernel_cols, precision=lax.Precision.HIGHEST)
    return result.reshape(grid_field.shape)


def smooth_tile(grid_field):
    padded = padded_2(grid_field, (("rows", 1),), HALF)
    rows_done = row_pass(padded, grid_field.shape[1])
    widened = padded_2(rows_done, (("maps", 2),), HALF)
    return column_pass(rows_done, widened[..., :HALF], widened[..., -HALF:])


def on_device(counts, weights):
    row_count = counts.shape[1]
    tile_width = counts.shape[2]
    cell_count = float(lax.axis_size("rows") * row_count * tile_width * lax.axis_size("maps"))
    smoothed = counts.astype(jnp.float32) + 1.0
    local_sums = jnp.sum(smoothed, axis=(1, 2))
    totals = lax.psum(local_sums, ("rows", "maps"))
    density = smoothed * (cell_count / totals)[:, None, None]
    mixing = weights / jnp.sum(weights)
    scaling = jnp.ones(density.shape, jnp.float32)
    barycenter = jnp.zeros((row_count, tile_width), jnp.float32)
    for iteration in range(ITERS):
        forward = smooth_tile(scaling)
        dual_scale = density / forward
        marginal = scaling * smooth_tile(dual_scale)
        barycenter = jnp.exp(jnp.sum(mixing[:, None, None] * jnp.log(marginal), axis=0))
        if iteration + 1 < ITERS:
            scaling = scaling * barycenter[None] / marginal
    return barycenter


def solution(mesh):
    in_specs = (P(None, "rows", "maps"), P())
    out_specs = P("rows", "maps")
    return jax.shard_map(
        on_device, mesh=mesh, in_specs=in_specs, out_specs=out_specs, check_vma=False
    )
```

profile of v0, /device:TPU:6, one launch (start us, length us, event | category | flops | bytes accessed | tf_op | source)
XLA Modules:
  0.0 682.2 jit_solution(16528823140833769040)
XLA Ops:
  6.6 4.4 fusion.65
  11.0 120.8 %psum.7 = f32[8]{0:T(128)S(1)} all-reduce(f32[8]{0:T(128)S(1)} %fusion.65), channel_id=1, replica_groups=mesh['rows'=16,'maps'=2] {'rows','maps'}, use_global_device_ids=true, to_apply=%region_2.0 | all-reduce | flops 8 | bytes 64 | tf_op jit(solution)/shard_map/psum | solution.py:68
  133.2 13.9 %fusion = f32[8,16384,16]{1,2,0:T(8,128)S(1)} fusion(f32[8,8,16384]{2,1,0:T(8,128)} %collective-permute-done.1, f32[8,16,16384]{2,1,0:T(8,128)S(1)} %broadcast.47, f32[8,8,16384]{2,1,0:T(8,128)} %collective-permute-done, f32[]{:T(128)} %fusion.132, s32[32]{0:T(128)S(1)} %iota_add_fusion.1), kind=kOutput, calls=%fused_computation | convolution fusion | flops 813699584 | bytes 25165956 | tf_op jit(solution)/shard_map/ij,mjc->mic/dot_general | solution.py:38
  148.5 5.0 collective-permute-start.3
  153.5 2.6 copy.44
  157.9 23.9 %fusion.24 = f32[8,16,64,256]{3,2,1,0:T(8,128)} fusion(f32[8,16,1,8]{3,2,1,0:T(1,128)S(1)} %bitcast.97, f32[8,16,63,8]{3,2,1,0:T(8,128)S(1)} %get-tuple-element.26, f32[8,16,64,256]{3,2,1,0:T(8,128)S(1)} %bitcast.85, f32[8,16,63,8]{3,2,1,0:T(8,128)S(1)} %get-tuple-element.25, f32[8,16,1,8]{3,2,1,0:T(1,128)S(1)} %bitcast.94, f32[]{:T(128)} %fusion.132, ...), kind=kOutput, calls=%fused_computation.24 | convolution fusion | flops 6854643712 | bytes 17302596 | tf_op jit(solution)/shard_map/mrbj,dj->mrbd/dot_general | solution.py:51
  181.8 9.5 %reshape.37 = f32[8,16,16384]{2,1,0:T(8,128)} reshape(f32[8,16,64,256]{3,2,1,0:T(8,128)} %fusion.24) | data formatting | bytes 16777216 | tf_op jit(solution)/shard_map/reshape | solution.py:52
  191.3 10.4 %fusion.67 = f32[8,16,16384]{2,1,0:T(8,128)} fusion(f32[8,16,16384]{2,1,0:T(8,128)} %reshape.37, s32[8,16,16384]{2,1,0:T(8,128)} %param.2, f32[8]{0:T(128)S(1)} %broadcast_divide_fusion.1), kind=kLoop, calls=%fused_computation.70 | loop fusion | flops 8388608 | bytes 25165856 | tf_op jit(solution)/shard_map/div | solution.py:75
  201.7 7.5 %fusion.173 = (f32[8,8,16384]{2,1,0:T(8,128)}, f32[8,8,16384]{2,1,0:T(8,128)}) fusion(f32[8,16,16384]{2,1,0:T(8,128)} %fusion.67), kind=kLoop, calls=%fused_computation.174 | loop fusion | bytes 16777216 | tf_op jit(solution)/shard_map/slice | solution.py:16
  211.1 3.6 collective-permute-start.5
  216.1 88.2 %collective-permute-done.4 = f32[8,8,16384]{2,1,0:T(8,128)} collective-permute-done((f32[8,8,16384]{2,1,0:T(8,128)}, f32[8,8,16384]{2,1,0:T(8,128)}, u32[]{:S(2)}, u32[]{:S(2)}) %collective-permute-start.4) | collective-permute-done | bytes 4194336 | tf_op jit(solution)/shard_map/ppermute | solution.py:18
  304.3 12.5 %fusion.6 = f32[8,16384,16]{1,2,0:T(8,128)S(1)} fusion(f32[8,8,16384]{2,1,0:T(8,128)} %collective-permute-done.5, f32[8,16,16384]{2,1,0:T(8,128)} %fusion.67, f32[8,8,16384]{2,1,0:T(8,128)} %collective-permute-done.4, f32[]{:T(128)} %fusion.132, s32[32]{0:T(128)S(1)} %iota_add_fusion.1), kind=kOutput, calls=%fused_computation.6 | convolution fusion | flops 813699584 | bytes 25165956 | tf_op jit(solution)/shard_map/ij,mjc->mic/dot_general | solution.py:38
  318.2 4.5 collective-permute-start.7
  322.7 2.6 copy.45
  325.4 3.7 fusion.172
  329.1 26.5 %multiply_reduce_fusion.1 = (f32[16,64,256]{2,1,0:T(8,128)S(1)}, f32[8,16,64,256]{3,2,1,0:T(8,128)}) fusion(f32[8]{0:T(128)S(1)} %broadcast_divide_fusion.2, f32[]{:T(128)} %fusion.132, s32[272]{0:T(512)S(1)} %iota_add_fusion, f32[8,16,1,8]{3,2,1,0:T(1,128)S(1)} %bitcast.96, f32[8,16,63,8]{3,2,1,0:T(8,128)} %get-tuple-element.20, ...), kind=kOutput, calls=%fused_computation.65 | convolution fusion | flops 6858575872 | bytes 18351204 | tf_op jit(solution)/shard_map/mrbj,dj->mrbd/dot_general | solution.py:51
  356.3 9.4 %reshape.39 = f32[8,16,16384]{2,1,0:T(8,128)} reshape(f32[8,16,64,256]{3,2,1,0:T(8,128)} %get-tuple-element.28) | data formatting | bytes 16777216 | tf_op jit(solution)/shard_map/reshape | solution.py:52
  365.7 4.9 broadcast_divide_fusion
  373.3 3.6 collective-permute-start.9
  376.9 89.2 %collective-permute-done.8 = f32[8,8,16384]{2,1,0:T(8,128)S(1)} collective-permute-done((f32[8,8,16384]{2,1,0:T(8,128)S(1)}, f32[8,8,16384]{2,1,0:T(8,128)S(1)}, u32[]{:S(2)}, u32[]{:S(2)}) %collective-permute-start.8) | collective-permute-done | bytes 4194336 | tf_op jit(solution)/shard_map/ppermute | solution.py:18
  466.1 11.9 %fusion.12 = f32[8,16384,16]{1,2,0:T(8,128)S(1)} fusion(f32[8,8,16384]{2,1,0:T(8,128)S(1)} %collective-permute-done.9, f32[8,16,16384]{2,1,0:T(8,128)S(1)} %broadcast_divide_fusion, f32[8,8,16384]{2,1,0:T(8,128)S(1)} %collective-permute-done.8, f32[]{:T(128)} %fusion.132, s32[32]{0:T(128)S(1)} %iota_add_fusion.1), kind=kOutput, calls=%fused_computation.12 | convolution fusion | flops 813699584 | bytes 25165956 | tf_op jit(solution)/shard_map/ij,mjc->mic/dot_general | solution.py:38
  479.4 4.7 collective-permute-start.11
  488.5 23.8 %fusion.44 = f32[8,16,64,256]{3,2,1,0:T(8,128)} fusion(f32[8,16,1,8]{3,2,1,0:T(1,128)S(1)} %bitcast.98, f32[8,16,63,8]{3,2,1,0:T(8,128)S(1)} %get-tuple-element.14, f32[8,16,64,256]{3,2,1,0:T(8,128)S(1)} %bitcast.87, f32[8,16,63,8]{3,2,1,0:T(8,128)S(1)} %get-tuple-element.13, f32[8,16,1,8]{3,2,1,0:T(1,128)S(1)} %bitcast.95, f32[]{:T(128)} %fusion.132, ...), kind=kOutput, calls=%fused_computation.44 | convolution fusion | flops 6854643712 | bytes 17302596 | tf_op jit(solution)/shard_map/mrbj,dj->mrbd/dot_general | solution.py:51
  512.3 9.8 %reshape.41 = f32[8,16,16384]{2,1,0:T(8,128)} reshape(f32[8,16,64,256]{3,2,1,0:T(8,128)} %fusion.44) | data formatting | bytes 16777216 | tf_op jit(solution)/shard_map/reshape | solution.py:52
  522.1 10.4 %fusion.66 = f32[8,16,16384]{2,1,0:T(8,128)} fusion(f32[8,16,16384]{2,1,0:T(8,128)} %reshape.41, s32[8,16,16384]{2,1,0:T(8,128)} %param.2, f32[8]{0:T(128)S(1)} %broadcast_divide_fusion.1), kind=kLoop, calls=%fused_computation.69 | loop fusion | flops 8388608 | bytes 25165856 | tf_op jit(solution)/shard_map/div | solution.py:75
  532.5 4.2 fusion.167
  538.8 3.6 collective-permute-start.13
  542.4 88.5 %collective-permute-done.12 = f32[8,8,16384]{2,1,0:T(8,128)S(1)} collective-permute-done((f32[8,8,16384]{2,1,0:T(8,128)S(1)}, f32[8,8,16384]{2,1,0:T(8,128)S(1)}, u32[]{:S(2)}, u32[]{:S(2)}) %collective-permute-start.12) | collective-permute-done | bytes 4194336 | tf_op jit(solution)/shard_map/ppermute | solution.py:18
  630.9 12.2 %fusion.18 = f32[8,16384,16]{1,2,0:T(8,128)S(1)} fusion(f32[8,8,16384]{2,1,0:T(8,128)S(1)} %collective-permute-done.13, f32[8,16,16384]{2,1,0:T(8,128)S(1)} %copy-done, f32[8,8,16384]{2,1,0:T(8,128)S(1)} %collective-permute-done.12, f32[]{:T(128)} %fusion.132, s32[32]{0:T(128)S(1)} %iota_add_fusion.1), kind=kOutput, calls=%fused_computation.18 | convolution fusion | flops 813699584 | bytes 25165956 | tf_op jit(solution)/shard_map/ij,mjc->mic/dot_general | solution.py:38
  644.5 4.7 collective-permute-start.15
  651.9 4.8 fusion.166
  656.6 23.6 %multiply_reduce_fusion = f32[16,64,256]{2,1,0:T(8,128)S(1)} fusion(f32[8,16,64,256]{3,2,1,0:T(8,128)} %get-tuple-element.28, f32[16,64,256]{2,1,0:T(8,128)S(1)} %exp.42, f32[8]{0:T(128)S(1)} %broadcast_divide_fusion.2, f32[8,16,1,8]{3,2,1,0:T(1,128)S(1)} %bitcast.93, f32[8,16,63,8]{3,2,1,0:T(8,128)} %get-tuple-element.8, ...), kind=kOutput, calls=%fused_computation.64 | convolution fusion | flops 6862770176 | bytes 19399780 | tf_op jit(solution)/shard_map/mrbj,dj->mrbd/dot_general | solution.py:51
  (47 shorter events, 32.6 us)
Async XLA Ops:
  2.3 130.1 %collective-permute-start.1 = (f32[8,8,16384]{2,1,0:T(8,128)}, f32[8,8,16384]{2,1,0:T(8,128)}, u32[]{:S(2)}, u32[]{:S(2)}) collective-permute-start(f32[8,8,16384]{2,1,0:T(8,128)} %broadcast.49), channel_id=1, source_target_pairs={{2,0},{4,2},{6,4},{8,6},{10,8},{12,10},{14,12},{16,14},{18,16},{20... | collective-permute-start | bytes 12582920 | tf_op jit(solution)/shard_map/ppermute | solution.py:19
  4.2 128.2 %collective-permute-start = (f32[8,8,16384]{2,1,0:T(8,128)}, f32[8,8,16384]{2,1,0:T(8,128)}, u32[]{:S(2)}, u32[]{:S(2)}) collective-permute-start(f32[8,8,16384]{2,1,0:T(8,128)} %broadcast.49), channel_id=1, source_target_pairs={{0,2},{2,4},{4,6},{6,8},{8,10},{10,12},{12,14},{14,16},{16,18},{18... | collective-permute-start | bytes 12582920 | tf_op jit(solution)/shard_map/ppermute | solution.py:18
  147.2 10.7 %collective-permute-start.2 = (f32[8,16,8]{2,1,0:T(8,128)S(1)}, f32[8,16,8]{2,1,0:T(8,128)S(1)}, u32[]{:S(2)}, u32[]{:S(2)}) collective-permute-start(f32[8,16,8]{2,1,0:T(8,128)S(1)} %get-tuple-element.23), channel_id=1, source_target_pairs={{0,1},{2,3},{4,5},{6,7},{8,9},{10,11},{12,13},{14,15},{16,17},{18,... | collective-permute-start | bytes 12296 | tf_op jit(solution)/shard_map/ppermute | solution.py:18
  148.5 9.4 %collective-permute-start.3 = (f32[8,16,8]{2,1,0:T(8,128)S(1)}, f32[8,16,8]{2,1,0:T(8,128)S(1)}, u32[]{:S(2)}, u32[]{:S(2)}) collective-permute-start(f32[8,16,8]{2,1,0:T(8,128)S(1)} %get-tuple-element.24), channel_id=1, source_target_pairs={{1,0},{3,2},{5,4},{7,6},{9,8},{11,10},{13,12},{15,14},{17,16},{19,... | collective-permute-start | bytes 12296 | tf_op jit(solution)/shard_map/ppermute | solution.py:19
  201.7 13.1 %copy-start.1 = (f32[8]{0:T(128)S(1)}, f32[8]{0:T(128)}, u32[]{:S(2)}) copy-start(f32[8]{0:T(128)} %param.3) | copy-start | bytes 100
  209.2 95.1 %collective-permute-start.4 = (f32[8,8,16384]{2,1,0:T(8,128)}, f32[8,8,16384]{2,1,0:T(8,128)}, u32[]{:S(2)}, u32[]{:S(2)}) collective-permute-start(f32[8,8,16384]{2,1,0:T(8,128)} %get-tuple-element.21), channel_id=1, source_target_pairs={{0,2},{2,4},{4,6},{6,8},{8,10},{10,12},{12,14},{14,16},{16,18},{18... | collective-permute-start | bytes 12582920 | tf_op jit(solution)/shard_map/ppermute | solution.py:18
  211.1 93.2 %collective-permute-start.5 = (f32[8,8,16384]{2,1,0:T(8,128)}, f32[8,8,16384]{2,1,0:T(8,128)}, u32[]{:S(2)}, u32[]{:S(2)}) collective-permute-start(f32[8,8,16384]{2,1,0:T(8,128)} %get-tuple-element.22), channel_id=1, source_target_pairs={{2,0},{4,2},{6,4},{8,6},{10,8},{12,10},{14,12},{16,14},{18,16},{20... | collective-permute-start | bytes 12582920 | tf_op jit(solution)/shard_map/ppermute | solution.py:19
  316.9 12.2 %collective-permute-start.6 = (f32[8,16,8]{2,1,0:T(8,128)S(1)}, f32[8,16,8]{2,1,0:T(8,128)S(1)}, u32[]{:S(2)}, u32[]{:S(2)}) collective-permute-start(f32[8,16,8]{2,1,0:T(8,128)S(1)} %get-tuple-element.17), channel_id=1, source_target_pairs={{0,1},{2,3},{4,5},{6,7},{8,9},{10,11},{12,13},{14,15},{16,17},{18,... | collective-permute-start | bytes 12296 | tf_op jit(solution)/shard_map/ppermute | solution.py:18
  318.2 10.9 %collective-permute-start.7 = (f32[8,16,8]{2,1,0:T(8,128)S(1)}, f32[8,16,8]{2,1,0:T(8,128)S(1)}, u32[]{:S(2)}, u32[]{:S(2)}) collective-permute-start(f32[8,16,8]{2,1,0:T(8,128)S(1)} %get-tuple-element.18), channel_id=1, source_target_pairs={{1,0},{3,2},{5,4},{7,6},{9,8},{11,10},{13,12},{15,14},{17,16},{19,... | collective-permute-start | bytes 12296 | tf_op jit(solution)/shard_map/ppermute | solution.py:19
  371.4 94.8 %collective-permute-start.8 = (f32[8,8,16384]{2,1,0:T(8,128)S(1)}, f32[8,8,16384]{2,1,0:T(8,128)S(1)}, u32[]{:S(2)}, u32[]{:S(2)}) collective-permute-start(f32[8,8,16384]{2,1,0:T(8,128)S(1)} %get-tuple-element.15), channel_id=1, source_target_pairs={{0,2},{2,4},{4,6},{6,8},{8,10},{10,12},{12,14},{14,16},{16,18},{18... | collective-permute-start | bytes 12582920 | tf_op jit(solution)/shard_map/ppermute | solution.py:18
  373.3 92.8 %collective-permute-start.9 = (f32[8,8,16384]{2,1,0:T(8,128)S(1)}, f32[8,8,16384]{2,1,0:T(8,128)S(1)}, u32[]{:S(2)}, u32[]{:S(2)}) collective-permute-start(f32[8,8,16384]{2,1,0:T(8,128)S(1)} %get-tuple-element.16), channel_id=1, source_target_pairs={{2,0},{4,2},{6,4},{8,6},{10,8},{12,10},{14,12},{16,14},{18,16},{20... | collective-permute-start | bytes 12582920 | tf_op jit(solution)/shard_map/ppermute | solution.py:19
  478.1 10.4 %collective-permute-start.10 = (f32[8,16,8]{2,1,0:T(8,128)S(1)}, f32[8,16,8]{2,1,0:T(8,128)S(1)}, u32[]{:S(2)}, u32[]{:S(2)}) collective-permute-start(f32[8,16,8]{2,1,0:T(8,128)S(1)} %get-tuple-element.11), channel_id=1, source_target_pairs={{0,1},{2,3},{4,5},{6,7},{8,9},{10,11},{12,13},{14,15},{16,17},{18,... | collective-permute-start | bytes 12296 | tf_op jit(solution)/shard_map/ppermute | solution.py:18
  479.4 9.1 %collective-permute-start.11 = (f32[8,16,8]{2,1,0:T(8,128)S(1)}, f32[8,16,8]{2,1,0:T(8,128)S(1)}, u32[]{:S(2)}, u32[]{:S(2)}) collective-permute-start(f32[8,16,8]{2,1,0:T(8,128)S(1)} %get-tuple-element.12), channel_id=1, source_target_pairs={{1,0},{3,2},{5,4},{7,6},{9,8},{11,10},{13,12},{15,14},{17,16},{19,... | collective-permute-start | bytes 12296 | tf_op jit(solution)/shard_map/ppermute | solution.py:19
  532.5 98.4 %copy-start = (f32[8,16,16384]{2,1,0:T(8,128)S(1)}, f32[8,16,16384]{2,1,0:T(8,128)}, u32[]{:S(2)}) copy-start(f32[8,16,16384]{2,1,0:T(8,128)} %fusion.66) | copy-start | bytes 25165828
  536.7 94.2 %collective-permute-start.12 = (f32[8,8,16384]{2,1,0:T(8,128)S(1)}, f32[8,8,16384]{2,1,0:T(8,128)S(1)}, u32[]{:S(2)}, u32[]{:S(2)}) collective-permute-start(f32[8,8,16384]{2,1,0:T(8,128)S(1)} %get-tuple-element.9), channel_id=1, source_target_pairs={{0,2},{2,4},{4,6},{6,8},{8,10},{10,12},{12,14},{14,16},{16,18},{18... | collective-permute-start | bytes 12582920 | tf_op jit(solution)/shard_map/ppermute | solution.py:18
  538.8 92.1 %collective-permute-start.13 = (f32[8,8,16384]{2,1,0:T(8,128)S(1)}, f32[8,8,16384]{2,1,0:T(8,128)S(1)}, u32[]{:S(2)}, u32[]{:S(2)}) collective-permute-start(f32[8,8,16384]{2,1,0:T(8,128)S(1)} %get-tuple-element.10), channel_id=1, source_target_pairs={{2,0},{4,2},{6,4},{8,6},{10,8},{12,10},{14,12},{16,14},{18,16},{20... | collective-permute-start | bytes 12582920 | tf_op jit(solution)/shard_map/ppermute | solution.py:19
  643.2 13.4 %collective-permute-start.14 = (f32[8,16,8]{2,1,0:T(8,128)S(1)}, f32[8,16,8]{2,1,0:T(8,128)S(1)}, u32[]{:S(2)}, u32[]{:S(2)}) collective-permute-start(f32[8,16,8]{2,1,0:T(8,128)S(1)} %get-tuple-element.5), channel_id=1, source_target_pairs={{0,1},{2,3},{4,5},{6,7},{8,9},{10,11},{12,13},{14,15},{16,17},{18,... | collective-permute-start | bytes 12296 | tf_op jit(solution)/shard_map/ppermute | solution.py:18
  644.5 12.1 %collective-permute-start.15 = (f32[8,16,8]{2,1,0:T(8,128)S(1)}, f32[8,16,8]{2,1,0:T(8,128)S(1)}, u32[]{:S(2)}, u32[]{:S(2)}) collective-permute-start(f32[8,16,8]{2,1,0:T(8,128)S(1)} %get-tuple-element.6), channel_id=1, source_target_pairs={{1,0},{3,2},{5,4},{7,6},{9,8},{11,10},{13,12},{15,14},{17,16},{19,... | collective-permute-start | bytes 12296 | tf_op jit(solution)/shard_map/ppermute | solution.py:19
where the time goes:
time: 689 us; the launch traced here: 682 us
  waiting for transfers between devices  266 us (39%)
  matrix products  148 us (21%)
  blocking collectives  121 us (18%)
  local copies, waits for them, and re-layouts  69.4 us (10%)
  starting transfers between devices  45.3 us (7%)
  other arithmetic  32 us (5%)
    ppermute x8, waiting for transfers between devices, padded_2(): before = lax.ppermute(last, axis, up)  266 us
    psum x1, blocking collectives, on_device(): totals = lax.psum(local_sums, ('rows', 'maps'))  121 us
    dot_general x4, matrix products, column_pass(): jnp.einsum('mrbj,dj->mrbd', extended, kernel_cols, precision=lax.Precisio...  97.8 us
    dot_general x4, matrix products, row_pass(): jnp.einsum('ij,mjc->mic', kernel_rows, padded, precision=lax.Precision.HI...  50.5 us
    ppermute x8, starting transfers between devices, padded_2(): after = lax.ppermute(first, axis, down)  31.8 us
    reshape x3, local copies, waits for them, and re-layouts, column_pass(): return result.reshape(grid_field.shape)  28.7 us
    div x2, other arithmetic, on_device(): dual_scale = density / forward  20.8 us
  transfers between devices with their start and end apart: 16, of which 3 were waited for; matrix products, arithmetic and copies ran while one was open for 4% of the time, Pallas kernels for 0%

commit v1 on v0

v1 whole, which is shorter than its diff:
```python
import functools

import jax
import jax.numpy as jnp
import ml_dtypes
import numpy as np
from jax import lax
from jax.experimental import pallas as pl
from jax.experimental.pallas import tpu as pltpu
from jax.sharding import PartitionSpec as P

HALF = 8
GROUP = 4
EDGE = 128
CHUNK = 256
LAG = 1
MESH = pl.DeviceIdType.MESH


def taps():
    across = np.arange(-HALF, HALF + 1).astype(np.float32)
    spread = 0.45 * HALF
    shape_taps = np.exp(-across * across / np.float32(2.0 * spread * spread))
    return (shape_taps / shape_taps.sum()).astype(np.float32)


def tap_table(offset):
    table = np.zeros(offset.shape, np.float32)
    inside = np.abs(offset) <= HALF
    table[inside] = taps()[offset[inside] + HALF]
    return table


def split(table):
    high = table.astype(ml_dtypes.bfloat16)
    return high, (table - high.astype(np.float32)).astype(ml_dtypes.bfloat16)


def column_table():
    out_col = np.arange(CHUNK)[None, :]
    in_col = np.concatenate(
        [np.arange(CHUNK), np.arange(-EDGE, 0), np.arange(CHUNK, CHUNK + EDGE)]
    )[:, None]
    high, low = split(tap_table(in_col - out_col))
    return np.concatenate([high, high, low], axis=0)


def row_table(rows):
    padded = rows + 2 * HALF
    offset = np.arange(padded)[None, :] - HALF - np.arange(rows)[:, None]
    high, low = split(tap_table(offset))
    fill = -3 * padded % 256
    return np.concatenate([high, high, low, np.zeros((rows, fill), high.dtype)], axis=1)


def window_factor(position, length):
    g = taps()
    total = jnp.zeros(position.shape, jnp.float32)
    for a in range(-HALF, HALF + 1):
        there = (position + a >= 0) & (position + a < length)
        total = total + jnp.where(there, float(g[a + HALF]), 0.0)
    inside = (position >= 0) & (position < length)
    return jnp.where(inside, 1.0 / jnp.where(inside, total, 1.0), 0.0)


def kernel(
    height, width, counts, mix, col_table, row_tab, out,
    cnt, scal, dual, obuf, row_fac, col_fac,
    csend, crecv, esend, erecv, xsend, hsend, hrecv, osend, orecv,
):
    maps, band, tile = counts.shape
    own = tile // GROUP
    cols = own + 2 * EDGE
    chunks = cols // CHUNK
    rows = GROUP * band
    padded = rows + 2 * HALF
    r, x = lax.axis_index("rows"), lax.axis_index("maps")
    groups, x_count = lax.axis_size("rows") // GROUP, lax.axis_size("maps")
    q, p = r // GROUP, r % GROUP

    def peer(k):
        return lax.rem(p + k, GROUP)

    barrier = pltpu.get_barrier_semaphore()

    def greet(row, col):
        pl.semaphore_signal(barrier, inc=1, device_id=(row, col), device_id_type=MESH)

    for k in range(1, GROUP):
        greet(q * GROUP + peer(k), x)
    for there, row in ((q > 0, r - GROUP), (q < groups - 1, r + GROUP)):
        @pl.when(there)
        def _():
            greet(row, x)
    for there, col in ((x > 0, x - 1), (x < x_count - 1, x + 1)):
        @pl.when(there)
        def _():
            for b in range(GROUP):
                greet(q * GROUP + b, col)
    up, down = (q > 0).astype(jnp.int32), (q < groups - 1).astype(jnp.int32)
    left, right = (x > 0).astype(jnp.int32), (x < x_count - 1).astype(jnp.int32)
    pl.semaphore_wait(barrier, GROUP - 1 + up + down + GROUP * (left + right))

    def aligned(value, to):
        return pl.multiple_of(value, to)

    def band_rows(b):
        return pl.ds(aligned(HALF + band * b, HALF), band)

    def piece(source_col, target_col, size, b):
        src = counts.at[:, :, pl.ds(aligned(source_col, EDGE), size)]
        dst = cnt.at[:, band_rows(b), pl.ds(aligned(target_col, EDGE), size)]
        return src, dst

    def count_copy(k, source_col, target_col, size, b, send, recv):
        src, dst = piece(source_col, target_col, size, b)
        if k == 0:
            return pltpu.make_async_copy(src, dst, recv)
        return pltpu.make_async_remote_copy(
            src_ref=src, dst_ref=dst, send_sem=send, recv_sem=recv,
            device_id=(q * GROUP + peer(k), x), device_id_type=MESH,
        )

    def main_copy(k, j, target, b, where):
        send, recv = csend.at[j, k], crecv.at[j, b]
        start = target * own
        if where == 0:
            return count_copy(k, start, EDGE, EDGE, b, send, recv)
        if where == 1:
            return count_copy(
                k, start - EDGE + CHUNK * j, CHUNK * j, CHUNK, b, send, recv)
        return count_copy(k, start + own - EDGE, cols - 2 * EDGE, EDGE, b, send, recv)

    def edge_copy(k, side, target, b):
        source = target * own + (own if side else -EDGE)
        return count_copy(
            k, source, (cols - EDGE) if side else 0, EDGE, b,
            esend.at[side, k], erecv.at[side, b])

    def x_copy(side, target_x, b):
        src, dst = piece(0 if side else tile - EDGE, (cols - EDGE) if side else 0, EDGE, b)
        return pltpu.make_async_remote_copy(
            src_ref=src, dst_ref=dst, send_sem=xsend.at[side], recv_sem=erecv.at[side, b],
            device_id=(q * GROUP + (GROUP - 1 if side else 0), target_x),
            device_id_type=MESH,
        )

    def has_edge(target, side):
        return (target < GROUP - 1) if side else (target > 0)

    def send_edges(side):
        for k in (1, 2, 3, 0):
            @pl.when(has_edge(peer(k), side))
            def _():
                edge_copy(k, side, peer(k), p).start()
        @pl.when((x > 0) if side else (x < x_count - 1))
        def _():
            x_copy(side, x - 1 if side else x + 1, p).start()

    for k in (1, 2, 3, 0):
        main_copy(k, 0, peer(k), p, 0).start()
    send_edges(0)

    @pl.loop(1, chunks - 1)
    def _(j):
        for k in (1, 2, 3, 0):
            main_copy(k, j, peer(k), p, 1).start()

    for k in (1, 2, 3, 0):
        main_copy(k, chunks - 1, peer(k), p, 2).start()
    send_edges(1)

    row_pos = q * rows - HALF + lax.broadcasted_iota(jnp.int32, row_fac.shape, 0)
    row_fac[...] = window_factor(row_pos, height)
    col_pos = x * tile + p * own - EDGE + lax.broadcasted_iota(jnp.int32, col_fac.shape, 1)
    col_fac[...] = window_factor(col_pos, width)
    for there, first in ((q == 0, 0), (q == groups - 1, HALF + rows)):
        @pl.when(there)
        def _():
            for buf in (cnt, scal, dual):
                @pl.loop(0, maps)
                def _(m):
                    buf[m, first:first + HALF, :] = jnp.zeros((HALF, cols), buf.dtype)
    for there, first in (
        ((x == 0) & (p == 0), 0),
        ((x == x_count - 1) & (p == GROUP - 1), cols - EDGE),
    ):
        @pl.when(there)
        def _():
            for m in range(maps):
                cnt[m, HALF:HALF + rows, first:first + EDGE] = jnp.zeros((rows, EDGE), jnp.int32)

    def wait_edges(side):
        inner = has_edge(p, side)
        outer = jnp.logical_not(inner) & ((x < x_count - 1) if side else (x > 0))
        @pl.when(inner)
        def _():
            for k in range(GROUP):
                copy = edge_copy(k, side, p, peer(k))
                copy.wait() if k == 0 else copy.wait_recv()
        @pl.when(outer)
        def _():
            for b in range(GROUP):
                x_copy(side, x + 1 if side else x - 1, b).wait_recv()

    def wait_counts(j):
        def wait(where):
            for k in range(GROUP):
                copy = main_copy(k, j, p, peer(k), where)
                copy.wait() if k == 0 else copy.wait_recv()
        @pl.when(j == 0)
        def _():
            wait(0)
            wait_edges(0)
        @pl.when((j > 0) & (j < chunks - 1))
        def _():
            wait(1)
        @pl.when(j == chunks - 1)
        def _():
            wait(2)
            wait_edges(1)

    def halo_copy(stage, j, way):
        buf = (cnt, scal, dual)[stage]
        source, target = ((rows, 0) if way else (HALF, HALF + rows))
        lanes = pl.ds(aligned(CHUNK * j, CHUNK), CHUNK)
        return pltpu.make_async_remote_copy(
            src_ref=buf.at[:, pl.ds(source, HALF), lanes],
            dst_ref=buf.at[:, pl.ds(target, HALF), lanes],
            send_sem=hsend.at[stage, j, way], recv_sem=hrecv.at[stage, j, way],
            device_id=(r + GROUP if way else r - GROUP, x), device_id_type=MESH,
        )

    def send_halo(stage, j):
        @pl.when(q > 0)
        def _():
            halo_copy(stage, j, 0).start()
        @pl.when(q < groups - 1)
        def _():
            halo_copy(stage, j, 1).start()

    def wait_halo(stage, j):
        @pl.when((j >= 0) & (j < chunks))
        def _():
            @pl.when(q < groups - 1)
            def _():
                halo_copy(stage, j, 0).wait_recv()
            @pl.when(q > 0)
            def _():
                halo_copy(stage, j, 1).wait_recv()

    def halves(value):
        high = value.astype(jnp.bfloat16)
        return high, (value - high.astype(jnp.float32)).astype(jnp.bfloat16)

    def smooth(load, start):
        before = jnp.maximum(start - EDGE, 0)
        after = jnp.minimum(start + CHUNK, cols - EDGE)
        parts = [halves(load(aligned(s, EDGE))) for s in (start, start + EDGE, before, after)]
        high, low = [a for a, _ in parts], [b for _, b in parts]
        lhs = jnp.concatenate(high + low + high, axis=-1).reshape(maps * padded, 6 * CHUNK)
        across = jnp.dot(lhs, col_table[...], preferred_element_type=jnp.float32)
        high, low = halves(across.reshape(maps, padded, CHUNK))
        fill = jnp.zeros((row_tab.shape[1] - 3 * padded, CHUNK), jnp.bfloat16)
        return [
            jnp.dot(
                row_tab[...],
                jnp.concatenate([high[m], low[m], high[m], fill], axis=0),
                preferred_element_type=jnp.float32,
            )
            for m in range(maps)
        ]

    def load_first(s):
        factor = row_fac[...] * col_fac[0:1, pl.ds(s, EDGE)]
        return (cnt[:, :, pl.ds(s, EDGE)].astype(jnp.float32) + 1.0) * factor[None]

    def load_scal(s):
        return scal[:, :, pl.ds(s, EDGE)]

    def load_dual(s):
        return dual[:, :, pl.ds(s, EDGE)]

    def mean_log(logs):
        total = mix[0] * logs[0]
        for m in range(1, maps):
            total = total + mix[m] * logs[m]
        return total

    def stage_a(j):
        start = aligned(CHUNK * j, CHUNK)
        lanes = pl.ds(start, CHUNK)
        logs = [jnp.log(value) for value in smooth(load_first, start)]
        mean = mean_log(logs)
        inside = jnp.broadcast_to(col_fac[0:1, lanes], (rows, CHUNK)) > 0.0
        for m in range(maps):
            scal[m, HALF:HALF + rows, lanes] = jnp.where(inside, jnp.exp(mean - logs[m]), 0.0)

    def stage_b(j):
        start = aligned(CHUNK * j, CHUNK)
        lanes = pl.ds(start, CHUNK)
        forward = smooth(load_scal, start)
        inside = jnp.broadcast_to(col_fac[0:1, lanes], (rows, CHUNK)) > 0.0
        for m in range(maps):
            points = cnt[m, HALF:HALF + rows, lanes].astype(jnp.float32) + 1.0
            dual[m, HALF:HALF + rows, lanes] = jnp.where(inside, points / forward[m], 0.0)

    def out_copy(k, j, target, source):
        src = obuf.at[pl.ds(aligned(band * target, HALF), band),
                      pl.ds(aligned(CHUNK * j, CHUNK), CHUNK)]
        dst = out.at[:, pl.ds(aligned(own * source + CHUNK * j, CHUNK), CHUNK)]
        if k == 0:
            return pltpu.make_async_copy(src, dst, orecv.at[j, source])
        return pltpu.make_async_remote_copy(
            src_ref=src, dst_ref=dst, send_sem=osend.at[j, k], recv_sem=orecv.at[j, source],
            device_id=(q * GROUP + peer(k), x), device_id_type=MESH,
        )

    def stage_c(j):
        start = aligned(EDGE + CHUNK * j, EDGE)
        mean = mean_log([jnp.log(value) for value in smooth(load_dual, start)])
        obuf[:, pl.ds(aligned(CHUNK * j, CHUNK), CHUNK)] = jnp.exp(mean)
        for k in (1, 2, 3, 0):
            out_copy(k, j, peer(k), p).start()

    @pl.loop(0, chunks + 3 * LAG + 2)
    def _(t):
        @pl.when(t < chunks)
        def _():
            wait_counts(t)
            send_halo(0, t)

        a = t - LAG - 1
        wait_halo(0, a + 1)
        @pl.when((a >= 0) & (a < chunks))
        def _():
            stage_a(a)
            send_halo(1, a)

        b = a - LAG - 1
        wait_halo(1, b + 1)
        @pl.when((b >= 0) & (b < chunks))
        def _():
            stage_b(b)
            send_halo(2, b)

        c = b - LAG - 1
        wait_halo(2, c + 1)
        @pl.when((c >= 0) & (c < chunks - 1))
        def _():
            stage_c(c)

    for k in range(1, GROUP):
        main_copy(k, 0, peer(k), p, 0).wait_send()
        main_copy(k, chunks - 1, peer(k), p, 2).wait_send()
        for side in range(2):
            @pl.when(has_edge(peer(k), side))
            def _():
                edge_copy(k, side, peer(k), p).wait_send()
    for side in range(2):
        @pl.when((x > 0) if side else (x < x_count - 1))
        def _():
            x_copy(side, x - 1 if side else x + 1, p).wait_send()

    @pl.loop(1, chunks - 1)
    def _(j):
        for k in range(1, GROUP):
            main_copy(k, j, peer(k), p, 1).wait_send()

    @pl.loop(0, chunks)
    def _(j):
        for stage in range(3):
            @pl.when(q > 0)
            def _():
                halo_copy(stage, j, 0).wait_send()
            @pl.when(q < groups - 1)
            def _():
                halo_copy(stage, j, 1).wait_send()

    @pl.loop(0, chunks - 1)
    def _(j):
        out_copy(0, j, p, p).wait()
        for k in range(1, GROUP):
            out_copy(k, j, peer(k), p).wait_send()
            out_copy(k, j, p, peer(k)).wait_recv()


def on_device(counts, weights):
    maps, band, tile = counts.shape
    height, width = lax.axis_size("rows") * band, lax.axis_size("maps") * tile
    own = tile // GROUP
    cols = own + 2 * EDGE
    chunks = cols // CHUNK
    rows = GROUP * band
    padded = rows + 2 * HALF

    points = jnp.sum(counts + 1, axis=(1, 2)).astype(jnp.float32)
    totals = lax.psum(points, ("rows", "maps"))
    mixing = weights / jnp.sum(weights)

    col_table, row_tab = column_table(), row_table(rows)
    dma = pltpu.SemaphoreType.DMA
    vmem = pl.BlockSpec(memory_space=pltpu.VMEM)
    result = pl.pallas_call(
        functools.partial(kernel, height, width),
        out_shape=jax.ShapeDtypeStruct((band, tile), jnp.float32),
        in_specs=[
            pl.BlockSpec(memory_space=pl.ANY),
            pl.BlockSpec(memory_space=pltpu.SMEM),
            vmem,
            vmem,
        ],
        out_specs=pl.BlockSpec(memory_space=pl.ANY),
        scratch_shapes=[
            pltpu.VMEM((maps, padded, cols), jnp.int32),
            pltpu.VMEM((maps, padded, cols), jnp.float32),
            pltpu.VMEM((maps, padded, cols), jnp.float32),
            pltpu.VMEM((rows, own), jnp.float32),
            pltpu.VMEM((padded, EDGE), jnp.float32),
            pltpu.VMEM((8, cols), jnp.float32),
            dma((chunks, GROUP)),
            dma((chunks, GROUP)),
            dma((2, GROUP)),
            dma((2, GROUP)),
            dma((2,)),
            dma((3, chunks, 2)),
            dma((3, chunks, 2)),
            dma((chunks, GROUP)),
            dma((chunks, GROUP)),
        ],
        compiler_params=pltpu.CompilerParams(
            collective_id=0, has_side_effects=True, vmem_limit_bytes=56 * 1024 * 1024
        ),
        cost_estimate=pl.CostEstimate(
            flops=10**11, bytes_accessed=10**8, transcendentals=10**7
        ),
    )(counts, mixing, jnp.asarray(col_table), jnp.asarray(row_tab))

    scales = float(height * width) / totals
    return result * jnp.exp(jnp.sum(mixing * jnp.log(scales)))


def solution(mesh):
    in_specs = (P(None, "rows", "maps"), P())
    out_specs = P("rows", "maps")
    return jax.shard_map(
        on_device, mesh=mesh, in_specs=in_specs, out_specs=out_specs, check_vma=False
    )
```

time: 689 us -> 182 us (0.26)
  the two profiles are of different devices: /device:TPU:6 before, /device:TPU:0 now
where the time goes in v1:
time: 182 us
  Pallas kernels  129 us (71%)
  blocking collectives  42 us (23%)
  other arithmetic  9.67 us (5%)
    pallas_call x1, Pallas kernels, on_device(): pl.pallas_call(functools.partial(kernel, height, width), out_shape=jax.Sh...  129 us
    psum x1, blocking collectives, on_device(): totals = lax.psum(points, ('rows', 'maps'))  42 us
    reduce_sum x1, other arithmetic, on_device(): points = jnp.sum(counts + 1, axis=(1, 2)).astype(jnp.float32)  4.15 us

profile of v1, /device:TPU:0, one launch (start us, length us, event | category | flops | bytes accessed | tf_op | source)
XLA Modules:
  0.0 181.9 jit_solution(4343644574799729016)
XLA Ops:
  0.0 0.0 copy-start
  0.0 1.3 reduce_sum.27
  1.3 4.2 %add_reduce_fusion = s32[8]{0:T(128)S(1)} fusion(s32[8,16,16384]{2,1,0:T(8,128)} %counts.1), kind=kLoop, calls=%fused_computation | loop fusion | flops 4194296 | bytes 8388640 | tf_op jit(solution)/shard_map/reduce_sum | solution.py:397
  5.5 42.0 %psum.7 = f32[8]{0:T(128)S(1)} all-reduce(f32[8]{0:T(128)S(1)} %convert_element_type.3), channel_id=1, replica_groups=mesh['rows'=16,'maps'=2] {'rows','maps'}, use_global_device_ids=true, to_apply=%region_2.0 | all-reduce | flops 8 | bytes 64 | tf_op jit(solution)/shard_map/psum | solution.py:398
  47.5 0.0 copy-done
  47.5 1.9 %multiply_reduce_fusion = (f32[]{:T(128)}, f32[8]{0:T(128)}) fusion(f32[8]{0:T(128)S(1)} %psum.7, f32[8]{0:T(128)S(1)} %copy-done, f32[]{:T(128)} %reduce_sum.27), kind=kLoop, calls=%fused_computation.2 | loop fusion | flops 31 | bytes 104 | tf_op jit(solution)/shard_map/reduce_sum | solution.py:440
  50.2 129.4 %shard_map.46 = f32[16,16384]{1,0:T(8,128)} custom-call(s32[8,16,16384]{2,1,0:T(8,128)} %counts.1, f32[8]{0:T(128)} %get-tuple-element.6.mix, bf16[1536,256]{1,0:T(8,128)(2,1)} %constant.12.clone.col_table, bf16[64,256]{1,0:T(8,128)(2,1)} %constant.13.clone.row_tab), custom_call_target="tpu_custom_call" | custom-call | flops 99999997952 | bytes 100000000 | tf_op jit(solution)/shard_map/pallas_call | solution.py:404
  179.6 2.3 %broadcast_multiply_fusion = f32[16,16384]{1,0:T(8,128)} fusion(f32[16,16384]{1,0:T(8,128)} %shard_map.46, f32[]{:T(128)S(6)} %exp.3), kind=kLoop, calls=%fused_computation.1 | loop fusion | flops 262144 | bytes 2097156 | tf_op jit(solution)/shard_map/mul | solution.py:440
  (1 shorter events, 0.0 us)
Async XLA Ops:
  0.0 47.5 %copy-start = (f32[8]{0:T(128)S(1)}, f32[8]{0:T(128)}, u32[]{:S(2)}) copy-start(f32[8]{0:T(128)} %param.5) | copy-start | bytes 100

commit v2 on v1

--- a/solution.py
+++ b/solution.py
@@ -64,9 +64,10 @@
 
 
 def kernel(
-    height, width, counts, mix, col_table, row_tab, out,
+    height, width, counts, weights, col_table, row_tab, out, factor_out,
     cnt, scal, dual, obuf, row_fac, col_fac,
     csend, crecv, esend, erecv, xsend, hsend, hrecv, osend, orecv,
+    points, part, running, arrived, psend, precv, tsend, trecv,
 ):
     maps, band, tile = counts.shape
     own = tile // GROUP
@@ -81,6 +82,14 @@
     def peer(k):
         return lax.rem(p + k, GROUP)
 
+    doubling = [(0, 1 << i) for i in range(groups.bit_length() - 1)]
+    doubling += [(1, 1 << i) for i in range(x_count.bit_length() - 1)]
+
+    def partner(axis, step):
+        place = (q, x)[axis]
+        other = place + (1 - 2 * lax.rem(place // step, 2)) * step
+        return (other * GROUP + p, x) if axis == 0 else (r, other)
+
     barrier = pltpu.get_barrier_semaphore()
 
     def greet(row, col):
@@ -97,9 +106,12 @@
         def _():
             for b in range(GROUP):
                 greet(q * GROUP + b, col)
+    far = [(axis, step) for axis, step in doubling if step > 1]
+    for axis, step in far:
+        greet(*partner(axis, step))
     up, down = (q > 0).astype(jnp.int32), (q < groups - 1).astype(jnp.int32)
     left, right = (x > 0).astype(jnp.int32), (x < x_count - 1).astype(jnp.int32)
-    pl.semaphore_wait(barrier, GROUP - 1 + up + down + GROUP * (left + right))
+    pl.semaphore_wait(barrier, GROUP - 1 + len(far) + up + down + GROUP * (left + right))
 
     def aligned(value, to):
         return pl.multiple_of(value, to)
@@ -281,11 +293,68 @@
     def load_dual(s):
         return dual[:, :, pl.ds(s, EDGE)]
 
+    weight_sum = weights[0]
+    for m in range(1, maps):
+        weight_sum = weight_sum + weights[m]
+
     def mean_log(logs):
-        total = mix[0] * logs[0]
+        total = weights[0] * logs[0]
         for m in range(1, maps):
-            total = total + mix[m] * logs[m]
-        return total
+            total = total + weights[m] * logs[m]
+        return total * (1.0 / jnp.full((1, CHUNK), weight_sum, jnp.float32))
+
+    points[...] = jnp.zeros(points.shape, jnp.int32)
+
+    def add_points(j):
+        start = aligned(EDGE + CHUNK * j, EDGE)
+        for m in range(maps):
+            block = cnt[m, HALF:HALF + rows, pl.ds(start, CHUNK)] + 1
+            block = block[:, :EDGE] + block[:, EDGE:]
+            points[m] += jnp.sum(block.reshape(rows // 8, 8, EDGE), axis=0)
+
+    def part_copy(k, source):
+        return pltpu.make_async_remote_copy(
+            src_ref=part.at[source], dst_ref=part.at[source],
+            send_sem=psend.at[k], recv_sem=precv.at[source],
+            device_id=(q * GROUP + peer(k), x), device_id_type=MESH,
+        )
+
+    def doubling_copy(i):
+        return pltpu.make_async_remote_copy(
+            src_ref=running.at[i], dst_ref=arrived.at[i],
+            send_sem=tsend.at[i], recv_sem=trecv.at[i],
+            device_id=partner(*doubling[i]), device_id_type=MESH,
+        )
+
+    def totals_step(i):
+        if i == 0:
+            sums = jnp.concatenate(
+                [jnp.sum(points[m], axis=0, keepdims=True) for m in range(maps)], axis=0)
+            sums = jnp.sum(sums, axis=1, keepdims=True).astype(jnp.float32)
+            part[p] = jnp.broadcast_to(sums, (maps, EDGE))
+            for k in range(1, GROUP):
+                part_copy(k, p).start()
+            return
+        if i == 1:
+            for k in range(1, GROUP):
+                part_copy(k, peer(k)).wait_recv()
+            total = part[0]
+            for b in range(1, GROUP):
+                total = total + part[b]
+        else:
+            doubling_copy(i - 2).wait_recv()
+            total = running[i - 2] + arrived[i - 2]
+        if i <= len(doubling):
+            running[i - 1] = total
+            doubling_copy(i - 1).start()
+            return
+        which = lax.broadcasted_iota(jnp.int32, total.shape, 0)
+        mixing = jnp.zeros(total.shape, jnp.float32)
+        for m in range(maps):
+            mixing = jnp.where(which == m, weights[m], mixing)
+        mixing = mixing / jnp.full(total.shape, weight_sum, jnp.float32)
+        mean = jnp.sum(mixing * jnp.log(float(height * width) / total), axis=0, keepdims=True)
+        factor_out[...] = jnp.broadcast_to(jnp.exp(mean), factor_out.shape)
 
     def stage_a(j):
         start = aligned(CHUNK * j, CHUNK)
@@ -323,12 +392,20 @@
         for k in (1, 2, 3, 0):
             out_copy(k, j, peer(k), p).start()
 
-    @pl.loop(0, chunks + 3 * LAG + 2)
+    @pl.loop(0, chunks + max(3 * LAG + 2, len(doubling) + 1))
     def _(t):
         @pl.when(t < chunks)
         def _():
             wait_counts(t)
             send_halo(0, t)
+
+        @pl.when((t > 0) & (t < chunks))
+        def _():
+            add_points(t - 1)
+        for i in range(len(doubling) + 2):
+            @pl.when(t == chunks - 1 + i)
+            def _():
+                totals_step(i)
 
         a = t - LAG - 1
         wait_halo(0, a + 1)
@@ -361,6 +438,11 @@
         @pl.when((x > 0) if side else (x < x_count - 1))
         def _():
             x_copy(side, x - 1 if side else x + 1, p).wait_send()
+
+    for k in range(1, GROUP):
+        part_copy(k, p).wait_send()
+    for i in range(len(doubling)):
+        doubling_copy(i).wait_send()
 
     @pl.loop(1, chunks - 1)
     def _(j):
@@ -394,23 +476,25 @@
     rows = GROUP * band
     padded = rows + 2 * HALF
 
-    points = jnp.sum(counts + 1, axis=(1, 2)).astype(jnp.float32)
-    totals = lax.psum(points, ("rows", "maps"))
-    mixing = weights / jnp.sum(weights)
+    groups, x_count = lax.axis_size("rows") // GROUP, lax.axis_size("maps")
+    rounds = groups.bit_length() + x_count.bit_length() - 2
 
     col_table, row_tab = column_table(), row_table(rows)
     dma = pltpu.SemaphoreType.DMA
     vmem = pl.BlockSpec(memory_space=pltpu.VMEM)
-    result = pl.pallas_call(
+    result, factor = pl.pallas_call(
         functools.partial(kernel, height, width),
-        out_shape=jax.ShapeDtypeStruct((band, tile), jnp.float32),
+        out_shape=(
+            jax.ShapeDtypeStruct((band, tile), jnp.float32),
+            jax.ShapeDtypeStruct((maps, EDGE), jnp.float32),
+        ),
         in_specs=[
             pl.BlockSpec(memory_space=pl.ANY),
             pl.BlockSpec(memory_space=pltpu.SMEM),
             vmem,
             vmem,
         ],
-        out_specs=pl.BlockSpec(memory_space=pl.ANY),
+        out_specs=(pl.BlockSpec(memory_space=pl.ANY), vmem),
         scratch_shapes=[
             pltpu.VMEM((maps, padded, cols), jnp.int32),
             pltpu.VMEM((maps, padded, cols), jnp.float32),
@@ -427,6 +511,14 @@
             dma((3, chunks, 2)),
             dma((chunks, GROUP)),
             dma((chunks, GROUP)),
+            pltpu.VMEM((maps, 8, EDGE), jnp.int32),
+            pltpu.VMEM((GROUP, maps, EDGE), jnp.float32),
+            pltpu.VMEM((max(rounds, 1), maps, EDGE), jnp.float32),
+            pltpu.VMEM((max(rounds, 1), maps, EDGE), jnp.float32),
+            dma((GROUP,)),
+            dma((GROUP,)),
+            dma((max(rounds, 1),)),
+            dma((max(rounds, 1),)),
         ],
         compiler_params=pltpu.CompilerParams(
             collective_id=0, has_side_effects=True, vmem_limit_bytes=56 * 1024 * 1024
@@ -434,10 +526,9 @@
         cost_estimate=pl.CostEstimate(
             flops=10**11, bytes_accessed=10**8, transcendentals=10**7
         ),
-    )(counts, mixing, jnp.asarray(col_table), jnp.asarray(row_tab))
-
-    scales = float(height * width) / totals
-    return result * jnp.exp(jnp.sum(mixing * jnp.log(scales)))
+    )(counts, weights, jnp.asarray(col_table), jnp.asarray(row_tab))
+
+    return result * factor[0, 0]
 
 
 def solution(mesh):

time: 182 us -> 140 us (0.77)
  blocking collectives: 42 us -> 0 us
  Pallas kernels: 129 us -> 136 us
  other arithmetic: 9.67 us -> 2.9 us
    psum x1 -> x0, blocking collectives: 42 us -> none  [on_device(): totals = lax.psum(points, ('rows', 'maps'))]
    reduce_sum x3 -> x0, other arithmetic: 7.4 us -> none  [the longest x1 4.15 us: on_device(): points = jnp.sum(counts + 1, axis=(1, 2)).astype(jnp.float32)]
    pallas_call x1, Pallas kernels: 129 us -> 136 us  [on_device(): pl.pallas_call(functools.partial(kernel, height, width), out_shape=(jax.S...]
where the time goes in v2:
time: 140 us
  Pallas kernels  136 us (97%)
  other arithmetic  2.9 us (2%)
    pallas_call x1, Pallas kernels, on_device(): pl.pallas_call(functools.partial(kernel, height, width), out_shape=(jax.S...  136 us
    mul x1, other arithmetic, on_device(): return result * factor[0, 0]  2.9 us

profile of v2, /device:TPU:0, one launch (start us, length us, event | category | flops | bytes accessed | tf_op | source)
XLA Modules:
  0.0 140.0 jit_solution(15080041080350515947)
XLA Ops:
  0.0 135.9 %shard_map.46 = (f32[16,16384]{1,0:T(8,128)}, f32[8,128]{1,0:T(8,128)}) custom-call(s32[8,16,16384]{2,1,0:T(8,128)} %counts.1, f32[8]{0:T(128)} %weights.1, bf16[1536,256]{1,0:T(8,128)(2,1)} %constant.4.clone.col_table, bf16[64,256]{1,0:T(8,128)(2,1)} %constant.5.clone.row_tab), custom_call_target="tpu_custom_call" | custom-call | flops 99999997952 | bytes 100000000 | tf_op jit(solution)/shard_map/pallas_call | solution.py:485
  135.9 1.2 slice.3
  137.1 2.9 %broadcast_multiply_fusion = f32[16,16384]{1,0:T(8,128)} fusion(f32[16,16384]{1,0:T(8,128)} %get-tuple-element.7, f32[]{:T(128)} %bitcast), kind=kLoop, calls=%fused_computation | loop fusion | flops 262144 | bytes 2097156 | tf_op jit(solution)/shard_map/mul | solution.py:531
